TPU v7x, 32 devices: a whole 2x2x4 slice. The times are simulated.
32 devices in a mesh: row: 8 (over z, core), col: 4 (over y, x).
Axes of the slice: x: 2, y: 2, z: 4, core: 2. Of those that a mesh axis runs over, the one named last changes fastest.
Arguments:
- packed_tiles: bfloat16 [384, 128, 512], P('row', None, 'col'), may hold values from -6 to 6
- source_pick: int32 [8, 48], P('row'), may hold values from 0 to 47, each once within a row
- owner_place: int32 [8, 48], P('row'), may hold values from 0 to 47, each once within a row
- tile_orient: int32 [8, 48], P('row'), may hold values from 0 to 3
- w_panel: bfloat16 [2048, 6144], P('row', 'col'), may hold values from -0.125 to 0.125
Outputs:
- particle_hole: bfloat16 [12288, 6144], P('row', 'col')
Inputs may be any that keep to these rules, and one draw needn't show every extreme that they name: `source_pick`: each row is a permutation of the stored tiles' local indices. `owner_place`: each row is a permutation of the received items.
All inputs are finite; a program needn't handle non-finite values.
Results may differ from a plain program's by a relative error of at most 0.001.
Values may be sent and summed in bfloat16 or wider, within the bound.
A program may use at most 128 MiB of HBM per device.

v0:
```python
import jax
import jax.numpy as jnp
from jax import lax
from jax.sharding import PartitionSpec as P

VW = 768
KC = 512


def orient_tiles(tile_set, orient_codes):
    flipped = (jnp.remainder(orient_codes, 2) == 1)[:, None, None, None]
    negated = (orient_codes >= 2)[:, None, None, None]
    turned = jnp.where(flipped, jnp.swapaxes(tile_set, 1, 3), tile_set)
    return jnp.where(negated, -turned, turned)


def assemble(tile_set, blocks):
    tile_width = tile_set.shape[1]
    col_tiles = KC // tile_width
    row_tiles = tile_set.shape[0] // col_tiles
    tile_grid = tile_set.reshape(row_tiles, col_tiles, tile_width, blocks, tile_width)
    return tile_grid.transpose(0, 2, 3, 1, 4).reshape(
        row_tiles * tile_width, blocks * col_tiles * tile_width
    )


def antisymmetrize(product):
    height = product.shape[0]
    breadth = product.shape[1]
    blocked = product.reshape(height // VW, VW, breadth // VW, VW)
    return (blocked - blocked.transpose(0, 3, 2, 1)).reshape(height, breadth).astype(jnp.bfloat16)


def on_device(packed_tiles, source_pick, owner_place, tile_orient, w_panel):
    stored = packed_tiles.shape[0]
    tile_width = packed_tiles.shape[1]
    row_peers = lax.axis_size("row")
    peer_slots = stored // row_peers
    outgoing = jnp.take(packed_tiles, source_pick[0], axis=0)
    outgoing = outgoing.reshape(row_peers, peer_slots, tile_width, tile_width)
    incoming = lax.all_to_all(outgoing, "row", split_axis=0, concat_axis=0, tiled=True)
    incoming = incoming.reshape(stored, tile_width, tile_width)
    owner_tiles = jnp.take(incoming, owner_place[0], axis=0).reshape(
        stored, tile_width, 1, tile_width
    )
    lambda_block = assemble(orient_tiles(owner_tiles, tile_orient[0]), 1)
    full_panel = lax.all_gather(w_panel, "row", axis=0, tiled=True)
    product = jnp.dot(
        lax.all_gather(lambda_block, "col", axis=1, tiled=True),
        full_panel,
        preferred_element_type=jnp.float32,
    )
    return antisymmetrize(product)


def solution(mesh):
    in_specs = (
        P("row", None, "col"),
        P("row", None),
        P("row", None),
        P("row", None),
        P("row", "col"),
    )
    out_specs = P("row", "col")
    return jax.shard_map(
        on_device, mesh=mesh, in_specs=in_specs, out_specs=out_specs, check_vma=False
    )
```

profile of v0, /device:TPU:24, one launch (start us, length us, event | category | flops | bytes accessed | tf_op | source)
XLA Modules:
  0.0 239.0 jit_solution(2462752232457879758)
XLA Ops:
  6.5 0.0 all-gather.5.cloned.1.call-start
  6.5 0.7 all-gather.5.cloned.1.call-update
  7.3 0.7 compare_select_fusion.1
  7.9 0.0 copy-done
  7.9 0.8 gather_fusion
  8.8 1.4 broadcast_select_fusion.1
  10.2 5.2 %all-to-all-start = ((bf16[8,6,128,128]{3,2,1,0:T(8,128)(2,1)}), bf16[8,6,128,128]{3,2,1,0:T(8,128)(2,1)S(1)}, u32[]{:S(2)}, u32[]{:S(2)}) async-start(bf16[8,6,128,128]{3,2,1,0:T(8,128)(2,1)} %bitcast.42), calls=%async_computation | async-start | bytes 3145728 | tf_op jit(solution)/shard_map/all_to_all | solution.py:41
  15.4 0.0 all-gather.3.cloned.1.call-start
  15.5 75.2 %all-to-all-done = bf16[8,6,128,128]{3,2,1,0:T(8,128)(2,1)S(1)} async-done(((bf16[8,6,128,128]{3,2,1,0:T(8,128)(2,1)}), bf16[8,6,128,128]{3,2,1,0:T(8,128)(2,1)S(1)}, u32[]{:S(2)}, u32[]{:S(2)}) %all-to-all-start) | async-done | bytes 1572896 | tf_op jit(solution)/shard_map/all_to_all | solution.py:41
  90.7 1.1 copy-done.1
  91.8 2.3 gather_fusion.1
  94.1 1.4 fusion.1
  95.4 2.6 %copy.10 = bf16[48,128,1,128]{3,1,0,2:T(8,128)(2,1)} copy(bf16[48,128,1,128]{1,3,0,2:T(8,128)(2,1)} %fusion.1) | data formatting | bytes 3145728 | tf_op jit(solution)/shard_map/transpose | solution.py:13
  98.0 1.8 negate_select_fusion
  99.8 1.2 copy.11
  101.0 1.4 copy.16
  102.4 0.0 all-gather.3.cloned.1.call-update
  102.5 0.4 all-gather.5.cloned.1.call-done
  102.9 72.9 %all-gather.3.cloned.1.call-done = bf16[1536,2048]{1,0:T(8,128)(2,1)} async-done(((bf16[1536,512]{1,0:T(8,128)(2,1)}), bf16[1536,2048]{1,0:T(8,128)(2,1)}) %all-gather.3.cloned.1.call-update) | async-done | bytes 6291472 | tf_op jit(solution)/shard_map/all_gather | solution.py:49
  175.7 15.7 %fusion.4 = f32[1536,1536]{1,0:T(8,128)} fusion(bf16[1536,2048]{1,0:T(8,128)(2,1)} %all-gather.3.cloned.1.call-done, bf16[2048,1536]{1,0:T(8,128)(2,1)} %all-gather.5.cloned.1.call-done), kind=kOutput, calls=%fused_computation.22 | convolution fusion | flops 9663676416 | bytes 22020096 | tf_op jit(solution)/shard_map/dot_general | solution.py:48
  191.4 12.1 %reshape.61 = f32[2,768,2,768]{3,2,1,0:T(2,128)} reshape(f32[1536,1536]{1,0:T(8,128)} %fusion.4) | data formatting | bytes 18874368 | tf_op jit(solution)/shard_map/reshape | solution.py:30
  203.5 17.5 %copy.12 = f32[2,768,2,768]{1,2,3,0:T(2,128)} copy(f32[2,768,2,768]{3,2,1,0:T(2,128)} %reshape.61) | data formatting | bytes 18874368 | tf_op jit(solution)/shard_map/reshape | solution.py:30
  221.0 8.0 %fusion = bf16[2,768,2,768]{3,2,1,0:T(2,128)(2,1)S(1)} fusion(f32[2,768,2,768]{3,2,1,0:T(2,128)} %reshape.61, f32[2,768,2,768]{1,2,3,0:T(2,128)} %copy.12), kind=kLoop, calls=%fused_computation.3 | loop fusion | flops 4718592 | bytes 23592960 | tf_op jit(solution)/shard_map/convert_element_type | solution.py:31
  229.0 3.1 %copy.14 = bf16[192,8,2,768]{3,1,2,0:T(8,128)(2,1)} copy(bf16[192,8,2,768]{3,2,1,0:T(2,128)(2,1)S(1)} %bitcast.38) | data formatting | bytes 9437184
  (13 shorter events, 0.1 us)
Async XLA Ops:
  6.5 1.4 copy-start
  6.5 96.3 %all-gather.5.cloned.1.call-start = ((), (), s32[]{:S(2)}) async-start(), calls=%async_computation.2 | async-start | bytes 7077888 | tf_op jit(solution)/shard_map/all_gather | solution.py:47
  7.9 0.9 copy-start.4
  10.2 5.2 %copy-start.2 = (s32[1,48]{1,0:T(1,128)S(1)}, s32[1,48]{1,0:T(1,128)}, u32[]{:S(2)}) copy-start(s32[1,48]{1,0:T(1,128)} %param.9) | copy-start | bytes 580
  10.2 5.3 %copy-start.3 = (s32[1,48]{1,0:T(1,128)S(1)}, s32[1,48]{1,0:T(1,128)}, u32[]{:S(2)}) copy-start(s32[1,48]{1,0:T(1,128)} %param.10) | copy-start | bytes 580
  10.2 80.5 %all-to-all-start = ((bf16[8,6,128,128]{3,2,1,0:T(8,128)(2,1)}), bf16[8,6,128,128]{3,2,1,0:T(8,128)(2,1)S(1)}, u32[]{:S(2)}, u32[]{:S(2)}) async-start(bf16[8,6,128,128]{3,2,1,0:T(8,128)(2,1)} %bitcast.42), calls=%async_computation | async-start | bytes 3145728 | tf_op jit(solution)/shard_map/all_to_all | solution.py:41
  15.4 160.3 %all-gather.3.cloned.1.call-start = ((), (), s32[]{:S(2)}) async-start(), calls=%async_computation.1 | async-start | bytes 7864320 | tf_op jit(solution)/shard_map/all_gather | solution.py:49
  90.7 1.1 copy-start.1
Sparse Core Ops, SparseCore 0:
  9.0 93.8 all-gather.4
  104.7 70.9 all-gather.2
where the time goes:
time: 242 us; the launch traced here: 239 us
  waiting for transfers between devices  149 us (62%)
  local copies, waits for them, and re-layouts  42.2 us (17%)
  matrix products  15.7 us (6%)
  between operations  13.5 us (6%)
  other arithmetic  13.2 us (5%)
  starting transfers between devices  5.23 us (2%)
    all_to_all x1, waiting for transfers between devices, on_device(): lax.all_to_all(outgoing, 'row', split_axis=0, concat_axis=0, tiled=True)  75.2 us
    all_gather x1, waiting for transfers between devices, on_device(): lax.all_gather(lambda_block, 'col', axis=1, tiled=True)  72.9 us
    reshape x2, local copies, waits for them, and re-layouts, antisymmetrize(): blocked = product.reshape(height // VW, VW, breadth // VW, VW)  29.5 us
    dot_general x1, matrix products, on_device(): jnp.dot(lax.all_gather(lambda_block, 'col', axis=1, tiled=True), full_pan...  15.7 us
    convert_element_type x1, other arithmetic, antisymmetrize(): (blocked - blocked.transpose(0, 3, 2, 1)).reshape(height, breadth)  8.05 us
    unnamed x12, local copies, waits for them, and re-layouts  5.72 us
    all_to_all x1, starting transfers between devices, on_device(): lax.all_to_all(outgoing, 'row', split_axis=0, concat_axis=0, tiled=True)  5.23 us
  transfers between devices with their start and end apart: 3, of which 3 were waited for; matrix products, arithmetic and copies ran while one was open for 6% of the time, Pallas kernels for 0%

commit v1 on v0

v1 whole, which is shorter than its diff:
```python
import functools

import jax
import jax.numpy as jnp
from jax import lax
from jax.experimental import pallas as pl
from jax.experimental.pallas import tpu as pltpu
from jax.sharding import PartitionSpec as P

VW = 768
MESH = pl.DeviceIdType.MESH


def kernel(
    n_row, n_col, tiles_hbm, pick, place, orient, w_hbm, out_hbm,
    tiles, outgoing, incoming, lam, panel, prod, result,
    load_sem, out_sem, a_send, a_recv, p_send, p_recv, l_send, l_fwd, l_recv,
):
    row, col = lax.axis_index("row"), lax.axis_index("col")
    chip, core = row // 2, row % 2
    chips = n_row // 2
    sibling = chip * 2 + 1 - core
    wide = 2
    high = n_col // wide
    hi, lo = col // wide, col % wide

    stored, tw, _ = tiles.shape
    slots = stored // n_row
    depth = panel.shape[0] // n_row
    height, kc = lam.shape[1], lam.shape[2]
    half = height // 2
    v_tiles = kc // tw
    breadth = panel.shape[1]

    load_tiles = pltpu.make_async_copy(tiles_hbm, tiles, load_sem.at[0])
    load_tiles.start()
    own_rows = pl.ds(pl.multiple_of(row * depth, depth), depth)
    load_w = pltpu.make_async_copy(w_hbm, panel.at[own_rows], load_sem.at[1])
    load_w.start()

    def row_peer(p):
        return lax.rem(row + p, n_row)

    x_peers = [hi * wide + lax.rem(lo + p, wide) for p in range(1, wide)]
    y_peers = [lax.rem(hi + p, high) * wide + lo for p in range(1, high)]

    barrier = pltpu.get_barrier_semaphore()
    for p in range(1, n_row):
        pl.semaphore_signal(barrier, inc=1, device_id=(row_peer(p), col), device_id_type=MESH)
    for c in x_peers + y_peers:
        pl.semaphore_signal(barrier, inc=1, device_id=(row, c), device_id_type=MESH)

    load_tiles.wait()

    def choose(t, carry):
        outgoing[t] = tiles[pick[0, t]]
        return carry

    lax.fori_loop(0, stored, choose, 0)
    load_w.wait()
    pl.semaphore_wait(barrier, n_row - 1 + len(x_peers) + len(y_peers))

    def exchange(p):
        to = row_peer(p)
        return pltpu.make_async_remote_copy(
            src_ref=outgoing.at[pl.ds(to * slots, slots)],
            dst_ref=incoming.at[pl.ds(row * slots, slots)],
            send_sem=a_send.at[p],
            recv_sem=a_recv.at[p],
            device_id=(to, col),
            device_id_type=MESH,
        )

    for p in range(1, n_row):
        exchange(p).start()

    def pass_on(slot, way, to):
        rows = pl.ds(pl.multiple_of(slot * depth, depth), depth)
        return pltpu.make_async_remote_copy(
            src_ref=panel.at[rows],
            dst_ref=panel.at[rows],
            send_sem=p_send.at[slot, way],
            recv_sem=p_recv.at[slot],
            device_id=(to, col),
            device_id_type=MESH,
        )

    has_left, has_right = chip > 0, chip < chips - 1

    pass_on(row, 2, sibling).start()

    def keep(t, carry):
        incoming[row * slots + t] = outgoing[row * slots + t]
        return carry

    lax.fori_loop(0, slots, keep, 0)
    for p in range(1, n_row):
        exchange(p).wait()

    @pl.when(has_left)
    def _():
        pass_on(row, 0, row - 2).start()

    @pl.when(has_right)
    def _():
        pass_on(row, 1, row + 2).start()

    def assemble(u, carry):
        for v in range(v_tiles):
            o = u * v_tiles + v
            code = orient[0, o]
            tile = incoming[place[0, o]].astype(jnp.float32)
            turned = jnp.where(code % 2 == 1, tile.T, tile)
            turned = jnp.where(code >= 2, -turned, turned)
            lam[col, pl.ds(pl.multiple_of(u * tw, tw), tw), v * tw:(v + 1) * tw] = turned.astype(jnp.bfloat16)
        return carry

    lax.fori_loop(0, stored // v_tiles, assemble, 0)

    def spread(block, h, sem, to):
        part = lam.at[block, h * half:(h + 1) * half]
        return pltpu.make_async_remote_copy(
            src_ref=part,
            dst_ref=part,
            send_sem=sem,
            recv_sem=l_recv.at[block, h],
            device_id=(row, to),
            device_id_type=MESH,
        )

    sent = []
    for first in range(2):
        for n, c in enumerate(x_peers):
            sent.append(spread(col, first, l_send.at[n, first], c))
            sent[-1].start()
        for n, c in enumerate(y_peers):
            sent.append(spread(col, 1 - first, l_send.at[wide - 1 + n, 1 - first], c))
            sent[-1].start()

    def panel_step(t):
        @pl.when(chip >= t)
        def _():
            slot = row - 2 * t
            pass_on(slot, 1, row).wait_recv()

            @pl.when(has_right)
            def _():
                pass_on(slot, 1, row + 2).start()

            pass_on(slot, 2, sibling).start()

        @pl.when(chip + t < chips)
        def _():
            slot = row + 2 * t
            pass_on(slot, 0, row).wait_recv()

            @pl.when(has_left)
            def _():
                pass_on(slot, 0, row - 2).start()

            pass_on(slot, 2, sibling).start()

    panel_step(1)
    for n, c in enumerate(x_peers):
        spread(c, 0, l_send.at[0, 0], col).wait_recv()
        for m, d in enumerate(y_peers):
            sent.append(spread(c, 0, l_fwd.at[0, n, m], d))
            sent[-1].start()
    for m, c in enumerate(y_peers):
        spread(c, 1, l_send.at[0, 0], col).wait_recv()
        for n, d in enumerate(x_peers):
            sent.append(spread(c, 1, l_fwd.at[1, n, m], d))
            sent[-1].start()
    for t in range(2, chips):
        panel_step(t)
    for q in range(chips):
        pass_on(q * 2 + 1 - core, 2, sibling).wait_recv()
    for c in x_peers:
        spread(c, 1, l_send.at[0, 0], col).wait_recv()
    for c in y_peers:
        spread(c, 0, l_send.at[0, 0], col).wait_recv()
    for n in range(1, wide):
        for m in range(1, high):
            diag = lax.rem(hi + m, high) * wide + lax.rem(lo + n, wide)
            for h in range(2):
                spread(diag, h, l_send.at[0, 0], col).wait_recv()

    pairs_i, pairs_j = height // VW, breadth // VW
    strip = VW // 3

    def block_out(i, j):
        return pltpu.make_async_copy(
            result.at[pl.ds(pl.multiple_of(i * VW, VW), VW), pl.ds(pl.multiple_of(j * VW, VW), VW)],
            out_hbm.at[pl.ds(pl.multiple_of(i * VW, VW), VW), pl.ds(pl.multiple_of(j * VW, VW), VW)],
            out_sem.at[i * pairs_j + j],
        )

    def one(ij, carry):
        i, j = ij // pairs_j, ij % pairs_j
        across = pl.ds(pl.multiple_of(j * VW, VW), VW)
        for a in range(3):
            down = pl.ds(pl.multiple_of(i * VW + a * strip, strip), strip)
            total = None
            for g in range(n_col):
                term = jnp.dot(
                    lam[g, down, :], panel[g * kc:(g + 1) * kc, across],
                    preferred_element_type=jnp.float32,
                )
                total = term if total is None else total + term
            prod[a * strip:(a + 1) * strip, :] = total
        for a in range(3):
            down = pl.ds(pl.multiple_of(i * VW + a * strip, strip), strip)
            mirrored = prod[:, a * strip:(a + 1) * strip].T
            result[down, across] = (prod[a * strip:(a + 1) * strip, :] - mirrored).astype(jnp.bfloat16)
        block_out(i, j).start()
        return carry

    lax.fori_loop(0, pairs_i * pairs_j, one, 0)

    for copy in sent:
        copy.wait_send()
    pass_on(row, 2, sibling).wait_send()

    @pl.when(has_left)
    def _():
        pass_on(row, 0, row - 2).wait_send()

    @pl.when(has_right)
    def _():
        pass_on(row, 1, row + 2).wait_send()

    for t in range(1, chips):
        @pl.when(chip >= t)
        def _(t=t):
            @pl.when(has_right)
            def _():
                pass_on(row - 2 * t, 1, row + 2).wait_send()

            pass_on(row - 2 * t, 2, sibling).wait_send()

        @pl.when(chip + t < chips)
        def _(t=t):
            @pl.when(has_left)
            def _():
                pass_on(row + 2 * t, 0, row - 2).wait_send()

            pass_on(row + 2 * t, 2, sibling).wait_send()

    for i in range(pairs_i):
        for j in range(pairs_j):
            block_out(i, j).wait()


def on_device(n_row, n_col, packed_tiles, source_pick, owner_place, tile_orient, w_panel):
    stored, tw, _ = packed_tiles.shape
    depth, breadth = w_panel.shape
    k = depth * n_row
    kc = k // n_col
    height = stored // (kc // tw) * tw
    wide = 2
    high = n_col // wide
    dma = pltpu.SemaphoreType.DMA
    smem = pl.BlockSpec(memory_space=pltpu.SMEM)
    anywhere = pl.BlockSpec(memory_space=pl.ANY)
    return pl.pallas_call(
        functools.partial(kernel, n_row, n_col),
        out_shape=jax.ShapeDtypeStruct((height, breadth), jnp.bfloat16),
        in_specs=[anywhere, smem, smem, smem, anywhere],
        out_specs=anywhere,
        scratch_shapes=[
            pltpu.VMEM((stored, tw, tw), jnp.bfloat16),
            pltpu.VMEM((stored, tw, tw), jnp.bfloat16),
            pltpu.VMEM((stored, tw, tw), jnp.bfloat16),
            pltpu.VMEM((n_col, height, kc), jnp.bfloat16),
            pltpu.VMEM((k, breadth), jnp.bfloat16),
            pltpu.VMEM((VW, VW), jnp.float32),
            pltpu.VMEM((height, breadth), jnp.bfloat16),
            dma((2,)),
            dma(((height // VW) * (breadth // VW),)),
            dma((n_row,)),
            dma((n_row,)),
            dma((n_row, 3)),
            dma((n_row,)),
            dma((wide + high - 2, 2)),
            dma((2, wide - 1, high - 1)),
            dma((n_col, 2)),
        ],
        compiler_params=pltpu.CompilerParams(
            collective_id=0, has_side_effects=True, vmem_limit_bytes=56 * 2**20
        ),
        cost_estimate=pl.CostEstimate(
            flops=2 * height * breadth * k, bytes_accessed=4 * height * breadth, transcendentals=0
        ),
    )(packed_tiles, source_pick, owner_place, tile_orient, w_panel)


def solution(mesh):
    in_specs = (
        P("row", None, "col"),
        P("row", None),
        P("row", None),
        P("row", None),
        P("row", "col"),
    )
    return jax.shard_map(
        functools.partial(on_device, mesh.shape["row"], mesh.shape["col"]),
        mesh=mesh, in_specs=in_specs, out_specs=P("row", "col"), check_vma=False,
    )
```

time: 242 us -> 116 us (0.48)
  the two profiles are of different devices: /device:TPU:24 before, /device:TPU:1 now
where the time goes in v1:
time: 116 us
  Pallas kernels  111 us (96%)
  local copies, waits for them, and re-layouts  4.83 us (4%)
    pallas_call x1, Pallas kernels, on_device(): pl.pallas_call(functools.partial(kernel, n_row, n_col), out_shape=jax.Sha...  111 us
    unnamed x1, local copies, waits for them, and re-layouts  4.83 us

profile of v1, /device:TPU:1, one launch (start us, length us, event | category | flops | bytes accessed | tf_op | source)
XLA Modules:
  0.0 116.3 jit_solution(3522060579492386439)
XLA Ops:
  0.0 111.5 %shard_map.55 = bf16[1536,1536]{1,0:T(8,128)(2,1)} custom-call(bf16[48,128,128]{2,1,0:T(8,128)(2,1)} %tiles_hbm.1, s32[1,48]{1,0:T(1,128)} %pick.1, s32[1,48]{1,0:T(1,128)} %place.1, s32[1,48]{1,0:T(1,128)} %orient.1, bf16[256,1536]{1,0:T(8,128)(2,1)} %w_hbm.1), custom_call_target="tpu_custom_call" | custom-call | flops 9663676416 | bytes 9437184 | tf_op jit(solution)/shard_map/pallas_call | solution.py:265
  111.5 4.8 %copy.7 = bf16[1536,1536]{1,0:T(8,128)(2,1)} copy(bf16[1536,1536]{1,0:T(8,128)(2,1)} %shard_map.55) | data formatting | bytes 9437184

commit v2 on v0

v2 whole, which is shorter than its diff:
```python
import functools

import jax
import jax.numpy as jnp
from jax import lax
from jax.experimental import pallas as pl
from jax.experimental.pallas import tpu as pltpu
from jax.sharding import PartitionSpec as P

VW = 768
PIECES = 4
MESH = pl.DeviceIdType.MESH


def kernel(
    n_row, n_col, tiles_hbm, pick, place, orient, w_hbm, prod,
    tiles, outgoing, raw, lam, panel,
    load_sem, a_send, p_send, p_recv, l_send, l_fwd, l_recv,
):
    row, col = lax.axis_index("row"), lax.axis_index("col")
    chip, core = row // 2, row % 2
    chips = n_row // 2
    sibling = chip * 2 + 1 - core
    wide = 2
    high = n_col // wide
    hi, lo = col // wide, col % wide

    stored, tw, _ = tiles.shape
    slots = stored // n_row
    depth = panel.shape[0] // n_row
    height, kc = lam.shape[1], lam.shape[2]
    v_tiles = kc // tw
    breadth = panel.shape[1]
    piece = depth // PIECES

    load_tiles = pltpu.make_async_copy(tiles_hbm, tiles, load_sem.at[0])
    load_tiles.start()
    own_rows = pl.ds(pl.multiple_of(row * depth, depth), depth)
    load_w = pltpu.make_async_copy(w_hbm, panel.at[own_rows], load_sem.at[1])
    load_w.start()

    def row_peer(p):
        return lax.rem(row + p, n_row)

    own = (0, 0)
    x_peers = [(0, p) for p in range(1, wide)]
    y_peers = [(p, 0) for p in range(1, high)]
    diagonals = [(m, n) for n in range(1, wide) for m in range(1, high)]

    def col_of(at):
        return lax.rem(hi + at[0], high) * wide + lax.rem(lo + at[1], wide)

    def number(at):
        return at[0] * wide + at[1]

    barrier = pltpu.get_barrier_semaphore()
    for p in range(1, n_row):
        pl.semaphore_signal(barrier, inc=1, device_id=(row_peer(p), col), device_id_type=MESH)
    for c in x_peers + y_peers:
        pl.semaphore_signal(barrier, inc=1, device_id=(row, col_of(c)), device_id_type=MESH)

    load_tiles.wait()

    def choose(t, carry):
        outgoing[t] = tiles[pick[0, t]]
        return carry

    lax.fori_loop(0, stored, choose, 0)
    pl.semaphore_wait(barrier, n_row - 1 + len(x_peers) + len(y_peers))

    def exchange(p):
        to = row_peer(p)
        return pltpu.make_async_remote_copy(
            src_ref=outgoing.at[pl.ds(to * slots, slots)],
            dst_ref=raw[0].at[pl.ds(row * slots, slots)],
            send_sem=a_send.at[p],
            recv_sem=l_recv.at[0, row],
            device_id=(to, col),
            device_id_type=MESH,
        )

    def pass_on(slot, r, way, to):
        rows = pl.ds(pl.multiple_of(slot * depth + r * piece, piece), piece)
        return pltpu.make_async_remote_copy(
            src_ref=panel.at[rows],
            dst_ref=panel.at[rows],
            send_sem=p_send.at[slot, r, way],
            recv_sem=p_recv.at[slot, r],
            device_id=(to, col),
            device_id_type=MESH,
        )

    def spread(block, s, sem, to):
        there = number(((block[0] - to[0]) % high, (block[1] - to[1]) % wide))
        items = pl.ds(s * slots, slots)
        return pltpu.make_async_remote_copy(
            src_ref=raw[number(block)].at[items],
            dst_ref=raw[there].at[items],
            send_sem=sem,
            recv_sem=l_recv.at[there, s],
            device_id=(row, col_of(to)),
            device_id_type=MESH,
        )

    def arrived(block, s):
        spread(block, s, l_send.at[s, 0], own).wait_recv()

    has_left, has_right = chip > 0, chip < chips - 1

    def to_sides(act):
        for r in range(PIECES):
            @pl.when(has_left)
            def _(r=r):
                act(pass_on(row, r, 0, row - 2))

            @pl.when(has_right)
            def _(r=r):
                act(pass_on(row, r, 1, row + 2))

    def chips_at(t, act):
        if t == 0:
            act(chip)
            return

        @pl.when(chip >= t)
        def _():
            act(chip - t)

        @pl.when(chip + t < chips)
        def _():
            act(chip + t)

    def direct(t):
        def act(q):
            for k in range(2):
                s = q * 2 + k
                arrived(own, s)
                for n, c in enumerate(x_peers + y_peers):
                    spread(own, s, l_send.at[s, n], c).start()

        chips_at(t, act)

    def onward(t):
        def act(q):
            for n, c in enumerate(x_peers):
                arrived(c, q * 2)
                for m, d in enumerate(y_peers):
                    spread(c, q * 2, l_fwd.at[q * 2, n, m], d).start()
            for m, c in enumerate(y_peers):
                arrived(c, q * 2 + 1)
                for n, d in enumerate(x_peers):
                    spread(c, q * 2 + 1, l_fwd.at[q * 2 + 1, n, m], d).start()

        chips_at(t, act)

    def panel_step(t, r):
        @pl.when(chip >= t)
        def _():
            slot = row - 2 * t
            pass_on(slot, r, 1, row).wait_recv()

            @pl.when(has_right)
            def _():
                pass_on(slot, r, 1, row + 2).start()

            pass_on(slot, r, 2, sibling).start()

        @pl.when(chip + t < chips)
        def _():
            slot = row + 2 * t
            pass_on(slot, r, 0, row).wait_recv()

            @pl.when(has_left)
            def _():
                pass_on(slot, r, 0, row - 2).start()

            pass_on(slot, r, 2, sibling).start()

    def rest_of_neighbours():
        for s in range(n_row):
            for c in x_peers if s % 2 else y_peers:
                arrived(c, s)

    def rest_of_diagonals():
        for c in diagonals:
            for s in range(n_row):
                arrived(c, s)

    def assemble(block):
        g, items = col_of(block), raw[number(block)]

        def one(u, carry):
            for v in range(v_tiles):
                o = u * v_tiles + v
                code = orient[0, o]
                tile = items[place[0, o]].astype(jnp.float32)
                turned = jnp.where(code % 2 == 1, tile.T, tile)
                turned = jnp.where(code >= 2, -turned, turned)
                lam[g, pl.ds(pl.multiple_of(u * tw, tw), tw), v * tw:(v + 1) * tw] = turned.astype(jnp.bfloat16)
            return carry

        lax.fori_loop(0, height // tw, one, 0)

    for p in range(1, n_row):
        exchange(p).start()
    load_w.wait()
    to_sides(lambda copy: copy.start())
    for r in range(PIECES):
        pass_on(row, r, 2, sibling).start()

    def keep(t, carry):
        raw[0][row * slots + t] = outgoing[row * slots + t]
        return carry

    lax.fori_loop(0, slots, keep, 0)
    for n, c in enumerate(x_peers + y_peers):
        spread(own, row, l_send.at[row, n], c).start()
    arrived(own, sibling)
    for n, c in enumerate(x_peers + y_peers):
        spread(own, sibling, l_send.at[sibling, n], c).start()
    for t in range(1, chips - 1):
        direct(t)
    panel_step(1, 0)
    direct(chips - 1)
    panel_step(1, 1)
    onward(0)
    for r in range(2, PIECES):
        panel_step(1, r)
        onward(r - 1)
    for t in range(PIECES - 1, chips - 1):
        onward(t)
    assemble(own)
    onward(chips - 1)
    steps = [(t, r) for t in range(2, chips - 1) for r in range(PIECES)]
    for t, r in steps[:-1]:
        panel_step(t, r)
    rest_of_neighbours()
    for c in x_peers + y_peers:
        assemble(c)
    panel_step(*steps[-1])
    rest_of_diagonals()
    for c in diagonals:
        assemble(c)

    strip = VW // 3
    across_n = breadth // VW

    def multiply(q, first):
        for r in range(PIECES):
            pass_on(q * 2 + 1 - core, r, 2, sibling).wait_recv()

        def one(step, carry):
            i, j = step // across_n, step % across_n
            down = pl.ds(pl.multiple_of(i * strip, strip), strip)
            across = pl.ds(pl.multiple_of(j * VW, VW), VW)
            term = jnp.dot(
                lam[q, down, :], panel[pl.ds(pl.multiple_of(q * kc, kc), kc), across],
                preferred_element_type=jnp.float32,
            )
            prod[down, across] = term if first else prod[down, across] + term
            return carry

        lax.fori_loop(0, height // strip * across_n, one, 0)

    multiply(chip, True)
    for t in range(1, chips):
        if t == chips - 1:
            for r in range(PIECES):
                panel_step(t, r)
        chips_at(t, functools.partial(multiply, first=False))

    for p in range(1, n_row):
        exchange(p).wait_send()
    for s in range(n_row):
        for n in range(wide + high - 2):
            spread(own, s, l_send.at[s, n], own).wait_send()
        for n in range(wide - 1):
            for m in range(high - 1):
                spread(own, s, l_fwd.at[s, n, m], own).wait_send()
    to_sides(lambda copy: copy.wait_send())
    for r in range(PIECES):
        pass_on(row, r, 2, sibling).wait_send()
        for t in range(1, chips):
            @pl.when(chip >= t)
            def _(t=t, r=r):
                @pl.when(has_right)
                def _():
                    pass_on(row - 2 * t, r, 1, row + 2).wait_send()

                pass_on(row - 2 * t, r, 2, sibling).wait_send()

            @pl.when(chip + t < chips)
            def _(t=t, r=r):
                @pl.when(has_left)
                def _():
                    pass_on(row + 2 * t, r, 0, row - 2).wait_send()

                pass_on(row + 2 * t, r, 2, sibling).wait_send()


def antisymmetrize(prod, out):
    strip = out.shape[0]
    i, j, a = pl.program_id(0), pl.program_id(1), pl.program_id(2)
    across = pl.ds(pl.multiple_of(j * VW, VW), VW)
    straight = prod[pl.ds(pl.multiple_of(i * VW + a * strip, strip), strip), across]
    crossed = prod[pl.ds(pl.multiple_of(i * VW, VW), VW), pl.ds(pl.multiple_of(j * VW + a * strip, strip), strip)]
    out[...] = (straight - crossed.T).astype(out.dtype)


def on_device(n_row, n_col, packed_tiles, source_pick, owner_place, tile_orient, w_panel):
    stored, tw, _ = packed_tiles.shape
    depth, breadth = w_panel.shape
    k = depth * n_row
    kc = k // n_col
    assert kc == 2 * depth
    height = stored // (kc // tw) * tw
    wide = 2
    high = n_col // wide
    dma = pltpu.SemaphoreType.DMA
    smem = pl.BlockSpec(memory_space=pltpu.SMEM)
    vmem = pl.BlockSpec(memory_space=pltpu.VMEM)
    anywhere = pl.BlockSpec(memory_space=pl.ANY)
    prod = pl.pallas_call(
        functools.partial(kernel, n_row, n_col),
        out_shape=pltpu.VMEM((height, breadth), jnp.float32),
        in_specs=[anywhere, smem, smem, smem, anywhere],
        out_specs=vmem,
        scratch_shapes=[
            pltpu.VMEM((stored, tw, tw), jnp.bfloat16),
            pltpu.VMEM((stored, tw, tw), jnp.bfloat16),
            [pltpu.VMEM((stored, tw, tw), jnp.bfloat16)] * n_col,
            pltpu.VMEM((n_col, height, kc), jnp.bfloat16),
            pltpu.VMEM((k, breadth), jnp.bfloat16),
            dma((2,)),
            dma((n_row,)),
            dma((n_row, PIECES, 3)),
            dma((n_row, PIECES)),
            dma((n_row, wide + high - 2)),
            dma((n_row, wide - 1, high - 1)),
            dma((n_col, n_row)),
        ],
        compiler_params=pltpu.CompilerParams(
            collective_id=0, has_side_effects=True, vmem_limit_bytes=48 * 2**20
        ),
        cost_estimate=pl.CostEstimate(
            flops=2 * height * breadth * k, bytes_accessed=4 * height * breadth, transcendentals=0
        ),
    )(packed_tiles, source_pick, owner_place, tile_orient, w_panel)
    strips = 3
    return pl.pallas_call(
        antisymmetrize,
        grid=(height // VW, breadth // VW, strips),
        out_shape=jax.ShapeDtypeStruct((height, breadth), jnp.bfloat16),
        in_specs=[vmem],
        out_specs=pl.BlockSpec((VW // strips, VW), lambda i, j, a: (i * strips + a, j)),
        compiler_params=pltpu.CompilerParams(vmem_limit_bytes=16 * 2**20),
        cost_estimate=pl.CostEstimate(
            flops=height * breadth, bytes_accessed=2 * height * breadth, transcendentals=0
        ),
    )(prod)


def solution(mesh):
    in_specs = (
        P("row", None, "col"),
        P("row", None),
        P("row", None),
        P("row", None),
        P("row", "col"),
    )
    return jax.shard_map(
        functools.partial(on_device, mesh.shape["row"], mesh.shape["col"]),
        mesh=mesh, in_specs=in_specs, out_specs=P("row", "col"), check_vma=False,
    )
```

time: 242 us -> 102 us (0.42)
  waiting for transfers between devices: 149 us -> 0 us
  Pallas kernels: 0 us -> 101 us
  local copies, waits for them, and re-layouts: 42.2 us -> 0 us
  matrix products: 15.7 us -> 0 us
  between operations: 13.5 us -> 0.01 us
  other arithmetic: 13.2 us -> 0 us
  starting transfers between devices: 5.23 us -> 0 us
    pallas_call x0 -> x2, Pallas kernels: none -> 101 us  [the longest x1 94.9 us: on_device(): pl.pallas_call(functools.partial(kernel, n_row, n_col), out_shape=pltpu.V...]
    all_to_all x1 -> x0, waiting for transfers between devices: 75.2 us -> none  [on_device(): lax.all_to_all(outgoing, 'row', split_axis=0, concat_axis=0, tiled=True)]
    all_gather x2 -> x0, waiting for transfers between devices: 73.2 us -> none  [the longest x1 72.9 us: on_device(): lax.all_gather(lambda_block, 'col', axis=1, tiled=True)]
    reshape x2 -> x0, local copies, waits for them, and re-layouts: 29.5 us -> none  [antisymmetrize(): blocked = product.reshape(height // VW, VW, breadth // VW, VW)]
    dot_general x1 -> x0, matrix products: 15.7 us -> none  [on_device(): jnp.dot(lax.all_gather(lambda_block, 'col', axis=1, tiled=True), full_pan...]
    convert_element_type x1 -> x0, other arithmetic: 8.05 us -> none  [antisymmetrize(): (blocked - blocked.transpose(0, 3, 2, 1)).reshape(height, breadth)]
    unnamed x12 -> x0, local copies, waits for them, and re-layouts: 5.72 us -> none
    all_to_all x1 -> x0, starting transfers between devices: 5.23 us -> none  [on_device(): lax.all_to_all(outgoing, 'row', split_axis=0, concat_axis=0, tiled=True)]
  transfers between devices with their start and end apart: 3 -> 0, of which waited for: 3 -> 0; matrix products, arithmetic and copies ran while one was open for 6% -> 0% of each run, Pallas kernels for 0% -> 0%
where the time goes in v2:
time: 102 us; the launch traced here: 101 us
  Pallas kernels  101 us (99%)
    pallas_call x1, Pallas kernels, on_device(): pl.pallas_call(functools.partial(kernel, n_row, n_col), out_shape=pltpu.V...  94.9 us
    pallas_call x1, Pallas kernels, on_device(): pl.pallas_call(antisymmetrize, grid=(height // VW, breadth // VW, strips)...  6.43 us

profile of v2, /device:TPU:24, one launch (start us, length us, event | category | flops | bytes accessed | tf_op | source)
XLA Modules:
  0.0 101.3 jit_solution(7426396857171585000)
XLA Ops:
  0.0 94.9 %shard_map.55.prod = f32[1536,1536]{1,0:T(8,128)S(1)} custom-call(bf16[48,128,128]{2,1,0:T(8,128)(2,1)} %tiles_hbm.1, s32[1,48]{1,0:T(1,128)} %pick.1, s32[1,48]{1,0:T(1,128)} %place.1, s32[1,48]{1,0:T(1,128)} %orient.1, bf16[256,1536]{1,0:T(8,128)(2,1)} %w_hbm.1), custom_call_target="tpu_custom_call" | custom-call | flops 9663676416 | bytes 9437184 | tf_op jit(solution)/shard_map/pallas_call | solution.py:323
  94.9 6.4 %shard_map.56 = bf16[1536,1536]{1,0:T(8,128)(2,1)} custom-call(f32[1536,1536]{1,0:T(8,128)S(1)} %shard_map.55.prod), custom_call_target="tpu_custom_call" | custom-call | flops 2359296 | bytes 4718592 | tf_op jit(solution)/shard_map/pallas_call | solution.py:350

commit v3 on v2

--- a/solution.py
+++ b/solution.py
@@ -201,7 +201,7 @@
 
         lax.fori_loop(0, height // tw, one, 0)
 
-    for p in range(1, n_row):
+    for p in [*range(2, n_row - 1), 1, n_row - 1]:
         exchange(p).start()
     load_w.wait()
     to_sides(lambda copy: copy.start())
@@ -346,7 +346,7 @@
             flops=2 * height * breadth * k, bytes_accessed=4 * height * breadth, transcendentals=0
         ),
     )(packed_tiles, source_pick, owner_place, tile_orient, w_panel)
-    strips = 3
+    strips = 1
     return pl.pallas_call(
         antisymmetrize,
         grid=(height // VW, breadth // VW, strips),

time: 102 us -> 99.2 us (0.973)
  Pallas kernels: 101 us -> 99 us
    pallas_call x1, Pallas kernels: 6.43 us -> 4.14 us  [on_device(): pl.pallas_call(antisymmetrize, grid=(height // VW, breadth // VW, strips)...]
where the time goes in v3:
time: 99.2 us; the launch traced here: 99 us
  Pallas kernels  99 us (100%)
    pallas_call x1, Pallas kernels, on_device(): pl.pallas_call(functools.partial(kernel, n_row, n_col), out_shape=pltpu.V...  94.9 us
    pallas_call x1, Pallas kernels, on_device(): pl.pallas_call(antisymmetrize, grid=(height // VW, breadth // VW, strips)...  4.14 us

profile of v3, /device:TPU:24, one launch (start us, length us, event | category | flops | bytes accessed | tf_op | source)
XLA Modules:
  0.0 99.0 jit_solution(350714825397948357)
XLA Ops:
  0.0 94.9 %shard_map.55.prod = f32[1536,1536]{1,0:T(8,128)S(1)} custom-call(bf16[48,128,128]{2,1,0:T(8,128)(2,1)} %tiles_hbm.1, s32[1,48]{1,0:T(1,128)} %pick.1, s32[1,48]{1,0:T(1,128)} %place.1, s32[1,48]{1,0:T(1,128)} %orient.1, bf16[256,1536]{1,0:T(8,128)(2,1)} %w_hbm.1), custom_call_target="tpu_custom_call" | custom-call | flops 9663676416 | bytes 9437184 | tf_op jit(solution)/shard_map/pallas_call | solution.py:323
  94.9 4.1 %shard_map.56 = bf16[1536,1536]{1,0:T(8,128)(2,1)} custom-call(f32[1536,1536]{1,0:T(8,128)S(1)} %shard_map.55.prod), custom_call_target="tpu_custom_call" | custom-call | flops 2359296 | bytes 4718592 | tf_op jit(solution)/shard_map/pallas_call | solution.py:350
